TPU v7x, 32 devices: a whole 2x2x4 slice. The times are simulated.
32 devices in a mesh: ang: 4 (over y, x), strip: 8 (over z, core).
Axes of the slice: x: 2, y: 2, z: 4, core: 2. Of those that a mesh axis runs over, the one named last changes fastest.
Arguments:
- slab: bfloat16 [4, 2, 1024, 512], P('ang', None, 'strip'), may hold values from -6 to 6
- shear_taps: float32 [4, 4, 4], replicated, may hold values from -1.5 to 1.5
- band_offsets: int32 [4, 4], replicated, may hold values from -64 to 64
- probe: bfloat16 [2, 256, 256], replicated, may hold values from -6 to 6
- scan_rows: int32 [4, 32], P('ang', 'strip'), may hold values from 0 to 127
- scan_columns: int32 [4, 32], P('ang', 'strip'), may hold values from 0 to 256
- frame_counts: int32 [4, 8], P('ang', 'strip'), may hold values from 1 to 4, 16 in all within a row
- amplitudes: bfloat16 [4, 32, 256, 256], P('ang', 'strip'), may hold values from 0.19921875 to 4
Outputs:
- slab_grad: float32 [4, 2, 1024, 512], P('ang', None, 'strip')
Inputs may be any that keep to these rules, and one draw needn't show every extreme that they name: `frame_counts`: for every angle the counts over the 8 strips sum to 16, and some strip has exactly 4 frames.
All inputs are finite; a program needn't handle non-finite values. No bound on the sum of `frame_counts` on one device may be relied on, other than what follows from the above.
Results may differ from a plain program's by a relative error of at most 0.013.
Values may be sent and summed in bfloat16 or wider, within the bound.
A program may use at most 64 MiB of HBM per device.

v0:
```python
import functools
import math

import jax
import jax.numpy as jnp
import ml_dtypes
import numpy as np
from jax import lax
from jax.experimental import pallas as pl
from jax.experimental.pallas import tpu as pltpu
from jax.sharding import PartitionSpec as P

MESH = pl.DeviceIdType.MESH
BF = jnp.bfloat16
F32 = jnp.float32


def dft_blocks(length):
    index = np.arange(length)
    phase = (np.outer(index, index) % length).astype(np.float32) * np.float32(2.0 * math.pi / length)
    scale = np.float32(1.0 / math.sqrt(length))
    cosine = (np.cos(phase) * scale).astype(ml_dtypes.bfloat16)
    sine = (np.sin(phase) * scale).astype(ml_dtypes.bfloat16)
    return np.block([[cosine, sine], [-sine, cosine]])


def kernel(
    n, strips, chunks, *refs,
):
    inputs, out, held, rest = refs[:9], refs[9], refs[10:19], refs[19:]
    slab, taps, offsets, probe, scan_rows, scan_columns, counts, amplitudes, wf = held
    (
        load, wg, ga, gb,
        bands_f, bands_b, ext, acc, edges, edge_in, img, column_cut, row_cut, column_place, row_place,
        cut, placed,
        a_send, a_recv, h_send, h_recv, e_send, e_recv, b_send, b_recv,
    ) = rest
    loads = [
        pltpu.make_async_copy(inputs[i], held[i], load.at[i]) for i in range(len(inputs))
    ]
    for each in loads:
        each.start()
    rows, width = slab.shape[2], slab.shape[3]
    length = probe.shape[1]
    slots = amplitudes.shape[1]
    tap_count = taps.shape[0]
    size = rows // chunks
    ang = lax.axis_index("ang")
    strip = lax.axis_index("strip")
    has_up = strip > 0
    has_down = strip < strips - 1
    square = n == 4
    if square:
        ax, ay = ang % 2, ang // 2
        near_x, near_y = ay * 2 + (1 - ax), (1 - ay) * 2 + ax
        order = [ang, near_x, near_y, (1 - ay) * 2 + (1 - ax)]
        peers = [near_x, near_y]
    else:
        order = [(ang + n - k) % n for k in range(n)]
        peers = [(ang + k) % n for k in range(1, n)]

    barrier = pltpu.get_barrier_semaphore()
    for peer in peers:
        pl.semaphore_signal(barrier, inc=1, device_id=(peer, strip), device_id_type=MESH)

    @pl.when(has_up)
    def _():
        pl.semaphore_signal(barrier, inc=1, device_id=(ang, strip - 1), device_id_type=MESH)

    @pl.when(has_down)
    def _():
        pl.semaphore_signal(barrier, inc=1, device_id=(ang, strip + 1), device_id_type=MESH)

    sides = (strip + strips - 1) // strips + 1 - (strip + 1) // strips
    pl.semaphore_wait(barrier, len(peers) + sides)

    def part(c):
        return pl.ds(c * size, size)

    def copy(src, dst, send, recv, device):
        return pltpu.make_async_remote_copy(
            src_ref=src, dst_ref=dst, send_sem=send, recv_sem=recv,
            device_id=device, device_id_type=MESH,
        )

    def gather_copy(own, g, send, recv, c, kind):
        if square and kind == 2:
            source, peer = (1, near_y) if c % 2 == 0 else (2, near_x)
            source = g.at[source, :, part(c), :]
        else:
            source, peer = own.at[:, part(c), :], peers[kind]
        return copy(
            source, g.at[kind + 1, :, part(c), :], send.at[kind, c], recv.at[kind, c], (peer, strip)
        )

    def gather_start(own, g, send, recv, c):
        for kind in range(len(peers)):
            gather_copy(own, g, send, recv, c, kind).start()

    def gather_forward(own, g, send, recv, c):
        if square:
            gather_copy(own, g, send, recv, c, c % 2).wait_recv()
            gather_copy(own, g, send, recv, c, 2).start()

    def gather_wait(own, g, send, recv, c):
        for kind in range(n - 1):
            if not (square and kind == c % 2):
                gather_copy(own, g, send, recv, c, kind).wait_recv()

    def gather_sent(own, g, send, recv):
        for c in range(chunks):
            for kind in range(n - 1):
                gather_copy(own, g, send, recv, c, kind).wait_send()

    def strip_copy(src, dst, send, recv, c, way):
        return copy(
            src.at[:, part(c), :], dst.at[way, :, part(c), :], send.at[way, c], recv.at[way, c],
            (ang, strip - 1 if way == 0 else strip + 1),
        )

    def halo_copy(c, way):
        target = 2 * rows if way == 0 else 0
        return copy(
            ext.at[:, pl.ds(rows + c * size, size), :],
            ext.at[:, pl.ds(target + c * size, size), :],
            h_send.at[way, c], h_recv.at[way, c], (ang, strip - 1 if way == 0 else strip + 1),
        )

    def band(k, sign, store):
        if sign > 0:
            angle, depth = ang, order[k]
        else:
            angle, depth = order[k], ang
        offset = offsets[angle, depth]
        weights = [taps[t, angle, depth] for t in range(tap_count)]
        step = 64

        @pl.loop(0, width // step)
        def _(i):
            shape = (step, width)
            source = lax.broadcasted_iota(jnp.int32, shape, 0) + i * step
            target = lax.broadcasted_iota(jnp.int32, shape, 1)
            tap = (source - target) * sign - offset
            value = jnp.zeros(shape, F32)
            for t in range(tap_count):
                value = jnp.where(tap == t, weights[t], value)
            store[k, pl.ds(pl.multiple_of(i * step, step), step), :] = value.astype(BF)

    def apply(own, g, bands, c):
        total = None
        for k in range(n):
            block = own[:, part(c), :] if k == 0 else g[k, :, part(c), :]
            term = jnp.dot(
                block.reshape(2 * size, width), bands[k], preferred_element_type=F32
            )
            total = term if total is None else total + term
        return total.reshape(2, size, width)

    def picks(shape, first, second, shift, live=None):
        hit = (
            lax.broadcasted_iota(jnp.int32, shape, second)
            - lax.broadcasted_iota(jnp.int32, shape, first)
        ) == shift
        if live is not None:
            hit = jnp.logical_and(hit, live)
        return jnp.where(hit, 1.0, 0.0).astype(BF)

    tall = length + rows
    frames = range(slots)
    middle = slice(rows, 2 * rows)
    above, below = slice(0, rows), slice(2 * rows, 3 * rows)

    def dot(left, right):
        return jnp.dot(left, right, preferred_element_type=F32)

    def span(f):
        return slice(f * length, (f + 1) * length)

    def prepare_cuts():
        for f in frames:
            column_cut[:, span(f)] = picks((width, length), 1, 0, scan_columns[0, f])
            row_cut[f] = picks((length, tall), 0, 1, scan_rows[0, f])

    def prepare_places():
        shape = (tall, length)
        for f in frames:
            column_place[f] = picks((length, width), 0, 1, scan_columns[0, f])
            live = lax.broadcasted_iota(jnp.int32, shape, 0) * 0 + f < counts[0, 0]
            row_place[:, span(f)] = picks(shape, 1, 0, scan_rows[0, f], live)
        wg[:length, :] = jnp.concatenate([wf[:length, :length], wf[length:, :length]], axis=1)
        wg[length:, :] = jnp.concatenate([wf[:length, length:], wf[:length, :length]], axis=1)

    def cut_columns(where):
        count = where.stop - where.start
        part_cut = dot(ext[:, where, :].reshape(2 * count, width), column_cut[...]).astype(BF)
        for f in frames:
            cut[f, where, :] = jnp.concatenate(
                [part_cut[:count, span(f)], part_cut[count:, span(f)]], axis=1
            )

    first = slab.at[0]
    loads[0].wait()
    for c in range(min(2, chunks)):
        gather_start(first, ga, a_send, a_recv, c)
    for i in (1, 2):
        loads[i].wait()
    for k in range(n):
        band(k, 1, bands_f)

    def finish(c):
        gather_wait(first, ga, a_send, a_recv, c)
        ext[:, pl.ds(rows + c * size, size), :] = apply(first, ga, bands_f, c).astype(BF)

        @pl.when(has_up)
        def _():
            halo_copy(c, 0).start()

        @pl.when(has_down)
        def _():
            halo_copy(c, 1).start()

    for c in range(chunks):
        gather_forward(first, ga, a_send, a_recv, c)
        if c + 2 < chunks:
            gather_start(first, ga, a_send, a_recv, c + 2)
        if c == 0:
            for each in loads[3:]:
                each.wait()
            prepare_cuts()
        elif c == 1:
            prepare_places()
        if c >= 1:
            finish(c - 1)
    finish(chunks - 1)
    cut_columns(middle)

    @pl.when(has_up)
    def _():
        for c in range(chunks):
            halo_copy(c, 1).wait_recv()

    @pl.when(jnp.logical_not(has_up))
    def _():
        ext[:, :rows, :] = jnp.zeros((2, rows, width), BF)

    @pl.when(has_down)
    def _():
        for c in range(chunks):
            halo_copy(c, 0).wait_recv()

    @pl.when(jnp.logical_not(has_down))
    def _():
        ext[:, 2 * rows :, :] = jnp.zeros((2, rows, width), BF)

    cut_columns(above)
    cut_columns(below)
    probe_real = probe[0].astype(F32)
    probe_imag = probe[1].astype(F32)

    def left(matrix, pair):
        both = dot(matrix[...], jnp.concatenate(pair, axis=0)).astype(BF)
        return jnp.concatenate([both[:length], both[length:]], axis=1)

    waves = []
    for f in frames:
        patch = dot(row_cut[f], cut[f])
        patch_real, patch_imag = patch[:, :length], patch[:, length:]
        waves.append(
            [
                (probe_real * patch_real - probe_imag * patch_imag).astype(BF),
                (probe_real * patch_imag + probe_imag * patch_real).astype(BF),
            ]
        )
    halves = [left(wf, wave) for wave in waves]
    residuals = []
    for f in frames:
        far = dot(halves[f], wg[...])
        far_real, far_imag = far[:, :length], far[:, length:]
        factor = 1.0 - amplitudes[0, f].astype(F32) * lax.rsqrt(
            far_real * far_real + far_imag * far_imag + 1.0
        )
        residuals.append([(far_real * factor).astype(BF), (far_imag * factor).astype(BF)])
    back_halves = [left(wg, residual) for residual in residuals]
    for f in frames:
        back = dot(back_halves[f], wf[...])
        back_real, back_imag = back[:, :length], back[:, length:]
        grad = jnp.concatenate(
            [
                (probe_real * back_real + probe_imag * back_imag).astype(BF),
                (probe_real * back_imag - probe_imag * back_real).astype(BF),
            ],
            axis=0,
        )
        wide = dot(grad, column_place[f]).astype(BF)
        placed[span(f), :] = jnp.concatenate([wide[:length], wide[length:]], axis=1)

    for way, where, here in ((0, above, has_up), (1, below, has_down)):
        edge = dot(row_place[where, :], placed[...]).astype(BF)
        edges[way, 0] = edge[:, :width]
        edges[way, 1] = edge[:, width:]

        @pl.when(here)
        def _(way=way):
            for c in range(chunks):
                strip_copy(edges.at[way], edge_in, e_send, e_recv, c, way).start()

    inner = dot(row_place[middle, :], placed[...])
    acc[0] = inner[:, :width]
    acc[1] = inner[:, width:]
    for k in range(n):
        band(k, -1, bands_b)
    for c in range(chunks):

        @pl.when(has_up)
        def _():
            strip_copy(edges.at[1], edge_in, e_send, e_recv, c, 1).wait_recv()
            acc[:, part(c), :] += edge_in[1, :, part(c), :].astype(F32)

        @pl.when(has_down)
        def _():
            strip_copy(edges.at[0], edge_in, e_send, e_recv, c, 0).wait_recv()
            acc[:, part(c), :] += edge_in[0, :, part(c), :].astype(F32)

        img[:, part(c), :] = acc[:, part(c), :].astype(BF)
        gather_start(img, gb, b_send, b_recv, c)
        if c >= 2:
            gather_forward(img, gb, b_send, b_recv, c - 2)
    for c in range(max(chunks - 2, 0), chunks):
        gather_forward(img, gb, b_send, b_recv, c)
    for c in range(chunks):
        gather_wait(img, gb, b_send, b_recv, c)
        out[0, :, part(c), :] = apply(img, gb, bands_b, c).astype(BF)

    gather_sent(first, ga, a_send, a_recv)
    gather_sent(img, gb, b_send, b_recv)
    for way, here in ((0, has_up), (1, has_down)):

        @pl.when(here)
        def _(way=way):
            for c in range(chunks):
                halo_copy(c, way).wait_send()
                strip_copy(edges.at[way], edge_in, e_send, e_recv, c, way).wait_send()


def per_device(
    n, strips, slab, shear_taps, band_offsets, probe, scan_rows, scan_columns, frame_counts, amplitudes
):
    rows, width = slab.shape[2], slab.shape[3]
    length = probe.shape[1]
    chunks = 4
    slots = amplitudes.shape[1]
    wf = dft_blocks(length)
    small = (1, 2, 4, 5, 6)
    operands = (
        slab, shear_taps, band_offsets, probe, scan_rows, scan_columns, frame_counts, amplitudes,
        jnp.asarray(wf),
    )
    dma = pltpu.SemaphoreType.DMA
    field = (2, rows, width)
    return pl.pallas_call(
        functools.partial(kernel, n, strips, chunks),
        out_shape=jax.ShapeDtypeStruct((1,) + field, BF),
        in_specs=[pl.BlockSpec(memory_space=pltpu.HBM)] * len(operands),
        out_specs=pl.BlockSpec(memory_space=pltpu.VMEM),
        scratch_shapes=[
            (pltpu.SMEM if i in small else pltpu.VMEM)(x.shape, x.dtype)
            for i, x in enumerate(operands)
        ]
        + [
            dma((len(operands),)),
            pltpu.VMEM(wf.shape, BF),
            pltpu.VMEM((n,) + field, BF),
            pltpu.VMEM((n,) + field, BF),
            pltpu.VMEM((n, width, width), BF),
            pltpu.VMEM((n, width, width), BF),
            pltpu.VMEM((2, length + rows, width), BF),
            pltpu.VMEM(field, F32),
            pltpu.VMEM((2,) + field, BF),
            pltpu.VMEM((2,) + field, BF),
            pltpu.VMEM(field, BF),
            pltpu.VMEM((width, slots * length), BF),
            pltpu.VMEM((slots, length, length + rows), BF),
            pltpu.VMEM((slots, length, width), BF),
            pltpu.VMEM((length + rows, slots * length), BF),
            pltpu.VMEM((slots, length + rows, 2 * length), BF),
            pltpu.VMEM((slots * length, 2 * width), BF),
            dma((n - 1, chunks)), dma((n - 1, chunks)),
            dma((2, chunks)), dma((2, chunks)),
            dma((2, chunks)), dma((2, chunks)),
            dma((n - 1, chunks)), dma((n - 1, chunks)),
        ],
        compiler_params=pltpu.CompilerParams(
            collective_id=0, has_side_effects=True, vmem_limit_bytes=62 << 20
        ),
    )(*operands).astype(F32)


def solution(mesh):
    return jax.shard_map(
        functools.partial(per_device, mesh.shape["ang"], mesh.shape["strip"]),
        mesh=mesh,
        in_specs=(
            P("ang", None, "strip", None),
            P(),
            P(),
            P(),
            P("ang", "strip"),
            P("ang", "strip"),
            P("ang", "strip"),
            P("ang", "strip", None, None),
        ),
        out_specs=P("ang", None, "strip", None),
        check_vma=False,
    )
```

profile of v0, /device:TPU:16, one launch (start us, length us, event | category | flops | bytes accessed | tf_op | source)
XLA Modules:
  0.0 43.3 jit_solution(15599558363896375431)
XLA Ops:
  0.7 40.9 %shard_map.91 = bf16[1,2,128,512]{3,2,1,0:T(8,128)(2,1)} custom-call(bf16[1,2,128,512]{3,2,1,0:T(8,128)(2,1)} %refs_0_.1, f32[4,4,4]{2,1,0:T(4,128)} %refs_1_.1, s32[4,4]{1,0:T(4,128)} %refs_2_.1, bf16[2,256,256]{2,1,0:T(8,128)(2,1)} %refs_3_.1, s32[1,4]{1,0:T(1,128)} %refs_4_.1, s32[1,4]{1,0:T(1,128)} %refs_5_.1, s32[1,1]{1,0:T(1,128)S(6)} %copy.10.refs_6_, ...), custom_call_target="tpu_custom_call" | custom-call | tf_op jit(solution)/shard_map/pallas_call | solution.py:360
  41.5 1.8 %convert_element_type.3 = f32[1,2,128,512]{3,2,1,0:T(8,128)} convert(bf16[1,2,128,512]{3,2,1,0:T(8,128)(2,1)} %shard_map.91) | non-fusion elementwise | flops 131072 | bytes 786432 | tf_op jit(solution)/shard_map/convert_element_type | solution.py:395
where the time goes:
time: 43.8 us; the launch traced here: 43.3 us
  Pallas kernels  40.9 us (93%)
  other arithmetic  1.8 us (4%)
  between operations  0.66 us (2%)
    pallas_call x1, Pallas kernels, per_device(): pl.pallas_call(functools.partial(kernel, n, strips, chunks), out_shape=ja...  40.9 us
    convert_element_type x1, other arithmetic, per_device(): return pl.pallas_call(functools.partial(kernel, n, strips, chunks), out_s...  1.8 us

commit v1 on v0

--- a/solution.py
+++ b/solution.py
@@ -102,10 +102,9 @@
             gather_copy(own, g, send, recv, c, c % 2).wait_recv()
             gather_copy(own, g, send, recv, c, 2).start()
 
-    def gather_wait(own, g, send, recv, c):
-        for kind in range(n - 1):
-            if not (square and kind == c % 2):
-                gather_copy(own, g, send, recv, c, kind).wait_recv()
+    def gather_wait(own, g, send, recv, c, kind):
+        if not (square and kind == c % 2):
+            gather_copy(own, g, send, recv, c, kind).wait_recv()
 
     def gather_sent(own, g, send, recv):
         for c in range(chunks):
@@ -146,9 +145,11 @@
                 value = jnp.where(tap == t, weights[t], value)
             store[k, pl.ds(pl.multiple_of(i * step, step), step), :] = value.astype(BF)
 
-    def apply(own, g, bands, c):
+    def apply(own, g, send, recv, bands, c):
         total = None
         for k in range(n):
+            if k > 0:
+                gather_wait(own, g, send, recv, c, k - 1)
             block = own[:, part(c), :] if k == 0 else g[k, :, part(c), :]
             term = jnp.dot(
                 block.reshape(2 * size, width), bands[k], preferred_element_type=F32
@@ -187,6 +188,8 @@
             column_place[f] = picks((length, width), 0, 1, scan_columns[0, f])
             live = lax.broadcasted_iota(jnp.int32, shape, 0) * 0 + f < counts[0, 0]
             row_place[:, span(f)] = picks(shape, 1, 0, scan_rows[0, f], live)
+
+    def prepare_transpose():
         wg[:length, :] = jnp.concatenate([wf[:length, :length], wf[length:, :length]], axis=1)
         wg[length:, :] = jnp.concatenate([wf[:length, length:], wf[:length, :length]], axis=1)
 
@@ -200,7 +203,7 @@
 
     first = slab.at[0]
     loads[0].wait()
-    for c in range(min(2, chunks)):
+    for c in range(min(3, chunks)):
         gather_start(first, ga, a_send, a_recv, c)
     for i in (1, 2):
         loads[i].wait()
@@ -208,8 +211,8 @@
         band(k, 1, bands_f)
 
     def finish(c):
-        gather_wait(first, ga, a_send, a_recv, c)
-        ext[:, pl.ds(rows + c * size, size), :] = apply(first, ga, bands_f, c).astype(BF)
+        piece = apply(first, ga, a_send, a_recv, bands_f, c)
+        ext[:, pl.ds(rows + c * size, size), :] = piece.astype(BF)
 
         @pl.when(has_up)
         def _():
@@ -221,18 +224,20 @@
 
     for c in range(chunks):
         gather_forward(first, ga, a_send, a_recv, c)
-        if c + 2 < chunks:
-            gather_start(first, ga, a_send, a_recv, c + 2)
+        if c + 3 < chunks:
+            gather_start(first, ga, a_send, a_recv, c + 3)
         if c == 0:
             for each in loads[3:]:
                 each.wait()
             prepare_cuts()
         elif c == 1:
-            prepare_places()
-        if c >= 1:
-            finish(c - 1)
-    finish(chunks - 1)
+            prepare_transpose()
+        else:
+            finish(c - 2)
+    for c in range(max(chunks - 2, 0), chunks):
+        finish(c)
     cut_columns(middle)
+    prepare_places()
 
     @pl.when(has_up)
     def _():
@@ -243,6 +248,8 @@
     def _():
         ext[:, :rows, :] = jnp.zeros((2, rows, width), BF)
 
+    cut_columns(above)
+
     @pl.when(has_down)
     def _():
         for c in range(chunks):
@@ -252,7 +259,6 @@
     def _():
         ext[:, 2 * rows :, :] = jnp.zeros((2, rows, width), BF)
 
-    cut_columns(above)
     cut_columns(below)
     probe_real = probe[0].astype(F32)
     probe_imag = probe[1].astype(F32)
@@ -328,8 +334,7 @@
     for c in range(max(chunks - 2, 0), chunks):
         gather_forward(img, gb, b_send, b_recv, c)
     for c in range(chunks):
-        gather_wait(img, gb, b_send, b_recv, c)
-        out[0, :, part(c), :] = apply(img, gb, bands_b, c).astype(BF)
+        out[0, :, part(c), :] = apply(img, gb, b_send, b_recv, bands_b, c)
 
     gather_sent(first, ga, a_send, a_recv)
     gather_sent(img, gb, b_send, b_recv)
@@ -359,7 +364,7 @@
     field = (2, rows, width)
     return pl.pallas_call(
         functools.partial(kernel, n, strips, chunks),
-        out_shape=jax.ShapeDtypeStruct((1,) + field, BF),
+        out_shape=pltpu.VMEM((1,) + field, F32),
         in_specs=[pl.BlockSpec(memory_space=pltpu.HBM)] * len(operands),
         out_specs=pl.BlockSpec(memory_space=pltpu.VMEM),
         scratch_shapes=[
@@ -392,7 +397,7 @@
         compiler_params=pltpu.CompilerParams(
             collective_id=0, has_side_effects=True, vmem_limit_bytes=62 << 20
         ),
-    )(*operands).astype(F32)
+    )(*operands)
 
 
 def solution(mesh):

time: 43.8 us -> 40.7 us (0.929)
  Pallas kernels: 40.9 us -> 38.9 us
  other arithmetic: 1.8 us -> 0 us
  local copies, waits for them, and re-layouts: 0 us -> 0.8 us
    pallas_call x1, Pallas kernels: 40.9 us -> 38.9 us  [per_device(): pl.pallas_call(functools.partial(kernel, n, strips, chunks), out_shape=pl...]
    convert_element_type x1 -> x0, other arithmetic: 1.8 us -> none  [per_device(): return pl.pallas_call(functools.partial(kernel, n, strips, chunks), out_s...]
    unnamed x0 -> x1, local copies, waits for them, and re-layouts: none -> 0.8 us
where the time goes in v1:
time: 40.7 us; the launch traced here: 40.4 us
  Pallas kernels  38.9 us (96%)
  local copies, waits for them, and re-layouts  0.8 us (2%)
  between operations  0.66 us (2%)
    pallas_call x1, Pallas kernels, per_device(): pl.pallas_call(functools.partial(kernel, n, strips, chunks), out_shape=pl...  38.9 us

profile of v1, /device:TPU:16, one launch (start us, length us, event | category | flops | bytes accessed | tf_op | source)
XLA Modules:
  0.0 40.4 jit_solution(14934011180373891088)
XLA Ops:
  0.7 38.9 %shard_map.91 = f32[1,2,128,512]{3,2,1,0:T(8,128)S(1)} custom-call(bf16[1,2,128,512]{3,2,1,0:T(8,128)(2,1)} %refs_0_.1, f32[4,4,4]{2,1,0:T(4,128)} %refs_1_.1, s32[4,4]{1,0:T(4,128)} %refs_2_.1, bf16[2,256,256]{2,1,0:T(8,128)(2,1)} %refs_3_.1, s32[1,4]{1,0:T(1,128)} %refs_4_.1, s32[1,4]{1,0:T(1,128)} %refs_5_.1, s32[1,1]{1,0:T(1,128)S(6)} %copy.12.refs_6_, ...), custom_call_target="tpu_custom_call" | custom-call | tf_op jit(solution)/shard_map/pallas_call | solution.py:365
  39.6 0.8 %copy.11 = f32[1,2,128,512]{3,2,1,0:T(8,128)} copy(f32[1,2,128,512]{3,2,1,0:T(8,128)S(1)} %shard_map.91) | data formatting | bytes 1048576

commit v2 on v1

--- a/solution.py
+++ b/solution.py
@@ -313,8 +313,7 @@
     inner = dot(row_place[middle, :], placed[...])
     acc[0] = inner[:, :width]
     acc[1] = inner[:, width:]
-    for k in range(n):
-        band(k, -1, bands_b)
+    built = 0
     for c in range(chunks):
 
         @pl.when(has_up)
@@ -329,10 +328,16 @@
 
         img[:, part(c), :] = acc[:, part(c), :].astype(BF)
         gather_start(img, gb, b_send, b_recv, c)
-        if c >= 2:
-            gather_forward(img, gb, b_send, b_recv, c - 2)
-    for c in range(max(chunks - 2, 0), chunks):
+        if c >= 1:
+            band(built, -1, bands_b)
+            built += 1
+    for c in range(chunks):
         gather_forward(img, gb, b_send, b_recv, c)
+        if built < n:
+            band(built, -1, bands_b)
+            built += 1
+    for k in range(built, n):
+        band(k, -1, bands_b)
     for c in range(chunks):
         out[0, :, part(c), :] = apply(img, gb, b_send, b_recv, bands_b, c)
 

time: 40.7 us -> 39.2 us (0.963)
  Pallas kernels: 38.9 us -> 37.1 us
    pallas_call x1, Pallas kernels: 38.9 us -> 37.1 us  [per_device(): pl.pallas_call(functools.partial(kernel, n, strips, chunks), out_shape=pl...]
where the time goes in v2:
time: 39.2 us; the launch traced here: 38.5 us
  Pallas kernels  37.1 us (95%)
  local copies, waits for them, and re-layouts  0.8 us (2%)
  between operations  0.66 us (2%)
    pallas_call x1, Pallas kernels, per_device(): pl.pallas_call(functools.partial(kernel, n, strips, chunks), out_shape=pl...  37.1 us
    unnamed x1, local copies, waits for them, and re-layouts  0.8 us

profile of v2, /device:TPU:16, one launch (start us, length us, event | category | flops | bytes accessed | tf_op | source)
XLA Modules:
  0.0 38.5 jit_solution(2157508676871989575)
XLA Ops:
  0.7 37.1 %shard_map.91 = f32[1,2,128,512]{3,2,1,0:T(8,128)S(1)} custom-call(bf16[1,2,128,512]{3,2,1,0:T(8,128)(2,1)} %refs_0_.1, f32[4,4,4]{2,1,0:T(4,128)} %refs_1_.1, s32[4,4]{1,0:T(4,128)} %refs_2_.1, bf16[2,256,256]{2,1,0:T(8,128)(2,1)} %refs_3_.1, s32[1,4]{1,0:T(1,128)} %refs_4_.1, s32[1,4]{1,0:T(1,128)} %refs_5_.1, s32[1,1]{1,0:T(1,128)S(6)} %copy.12.refs_6_, ...), custom_call_target="tpu_custom_call" | custom-call | tf_op jit(solution)/shard_map/pallas_call | solution.py:370
  37.7 0.8 %copy.11 = f32[1,2,128,512]{3,2,1,0:T(8,128)} copy(f32[1,2,128,512]{3,2,1,0:T(8,128)S(1)} %shard_map.91) | data formatting | bytes 1048576

commit v3 on v2

--- a/solution.py
+++ b/solution.py
@@ -31,7 +31,7 @@
     slab, taps, offsets, probe, scan_rows, scan_columns, counts, amplitudes, wf = held
     (
         load, wg, ga, gb,
-        bands_f, bands_b, ext, acc, edges, edge_in, img, column_cut, row_cut, column_place, row_place,
+        bands_f, bands_b, ext, acc, edges, edge_in, img, column_cut, w_rows, probe_rows, column_place, row_place,
         cut, placed,
         a_send, a_recv, h_send, h_recv, e_send, e_recv, b_send, b_recv,
     ) = rest
@@ -177,10 +177,18 @@
     def span(f):
         return slice(f * length, (f + 1) * length)
 
-    def prepare_cuts():
-        for f in frames:
+    def prepare_cuts(some):
+        for f in some:
             column_cut[:, span(f)] = picks((width, length), 1, 0, scan_columns[0, f])
-            row_cut[f] = picks((length, tall), 0, 1, scan_rows[0, f])
+            row_cut = picks((length, tall), 0, 1, scan_rows[0, f])
+            cosine = dot(wf[:length, :length], row_cut).astype(BF)
+            sine = dot(wf[:length, length:], row_cut).astype(BF)
+            w_rows[f, :length, :] = jnp.concatenate([cosine, sine], axis=1)
+            w_rows[f, length:, :] = jnp.concatenate([-sine, cosine], axis=1)
+            probe_rows[f] = dot(
+                picks((tall, length), 1, 0, scan_rows[0, f]),
+                jnp.concatenate([probe[0], probe[1]], axis=1),
+            ).astype(BF)
 
     def prepare_places():
         shape = (tall, length)
@@ -229,8 +237,9 @@
         if c == 0:
             for each in loads[3:]:
                 each.wait()
-            prepare_cuts()
+            prepare_cuts(frames[: slots // 2])
         elif c == 1:
+            prepare_cuts(frames[slots // 2 :])
             prepare_transpose()
         else:
             finish(c - 2)
@@ -269,15 +278,17 @@
 
     waves = []
     for f in frames:
-        patch = dot(row_cut[f], cut[f])
-        patch_real, patch_imag = patch[:, :length], patch[:, length:]
+        patch_real = cut[f, :, :length].astype(F32)
+        patch_imag = cut[f, :, length:].astype(F32)
+        here_real = probe_rows[f, :, :length].astype(F32)
+        here_imag = probe_rows[f, :, length:].astype(F32)
         waves.append(
             [
-                (probe_real * patch_real - probe_imag * patch_imag).astype(BF),
-                (probe_real * patch_imag + probe_imag * patch_real).astype(BF),
+                (here_real * patch_real - here_imag * patch_imag).astype(BF),
+                (here_real * patch_imag + here_imag * patch_real).astype(BF),
             ]
         )
-    halves = [left(wf, wave) for wave in waves]
+    halves = [left(w_rows.at[f], waves[f]) for f in frames]
     residuals = []
     for f in frames:
         far = dot(halves[f], wg[...])
@@ -389,7 +400,8 @@
             pltpu.VMEM((2,) + field, BF),
             pltpu.VMEM(field, BF),
             pltpu.VMEM((width, slots * length), BF),
-            pltpu.VMEM((slots, length, length + rows), BF),
+            pltpu.VMEM((slots, 2 * length, 2 * (length + rows)), BF),
+            pltpu.VMEM((slots, length + rows, 2 * length), BF),
             pltpu.VMEM((slots, length, width), BF),
             pltpu.VMEM((length + rows, slots * length), BF),
             pltpu.VMEM((slots, length + rows, 2 * length), BF),

time: 39.2 us -> 39.1 us (level)
  no operation moved by 1% of the time
where the time goes in v3:
time: 39.1 us; the launch traced here: 38.4 us
  Pallas kernels  37 us (95%)
  local copies, waits for them, and re-layouts  0.8 us (2%)
  between operations  0.66 us (2%)
    pallas_call x1, Pallas kernels, per_device(): pl.pallas_call(functools.partial(kernel, n, strips, chunks), out_shape=pl...  37 us
    unnamed x1, local copies, waits for them, and re-layouts  0.8 us

profile of v3, /device:TPU:16, one launch (start us, length us, event | category | flops | bytes accessed | tf_op | source)
XLA Modules:
  0.0 38.4 jit_solution(6232890815226186917)
XLA Ops:
  0.7 37.0 %shard_map.91 = f32[1,2,128,512]{3,2,1,0:T(8,128)S(1)} custom-call(bf16[1,2,128,512]{3,2,1,0:T(8,128)(2,1)} %refs_0_.1, f32[4,4,4]{2,1,0:T(4,128)} %refs_1_.1, s32[4,4]{1,0:T(4,128)} %refs_2_.1, bf16[2,256,256]{2,1,0:T(8,128)(2,1)} %refs_3_.1, s32[1,4]{1,0:T(1,128)} %refs_4_.1, s32[1,4]{1,0:T(1,128)} %refs_5_.1, s32[1,1]{1,0:T(1,128)S(6)} %copy.12.refs_6_, ...), custom_call_target="tpu_custom_call" | custom-call | tf_op jit(solution)/shard_map/pallas_call | solution.py:381
  37.6 0.8 %copy.11 = f32[1,2,128,512]{3,2,1,0:T(8,128)} copy(f32[1,2,128,512]{3,2,1,0:T(8,128)S(1)} %shard_map.91) | data formatting | bytes 1048576
